TPU v7x, 32 devices: a whole 2x2x4 slice. The times are simulated.
32 devices in a mesh: tile: 8 (over z, y), lev: 4 (over x, core).
Axes of the slice: x: 2, y: 2, z: 4, core: 2. Of those that a mesh axis runs over, the one named last changes fastest.
Arguments:
- cotangent: bfloat16 [3072, 128, 128], P('lev', 'tile'), may hold values from -6 to 6
- mix_weight: bfloat16 [3072, 3072], P(None, 'tile'), may hold values from -0.109375 to 0.109375
- kernel: float32 [3072, 9], P('lev'), may hold values from -2 to 2
- send_rows: int32 [8, 8, 41], P('tile'), may hold values from -1 to 291, as said below
- recv_cells: int32 [8, 8, 41], P('tile'), may hold values from -1 to 1918, as said below
- recv_weight: float32 [8, 4, 8, 41], P('tile'), may hold values from 0 to 1, as said below
Outputs:
- grad_input: bfloat16 [3072, 128, 128], P('lev', 'tile')
Inputs may be any that keep to these rules, and one draw needn't show every extreme that they name: `send_rows`: partner d is always a strip of the other panel. Every slot of the side columns (with the four corners) of strip s appears exactly once over all d and k, the slots of row 0 only for the strip at place 0 of a panel and those of row 17 only for the strip at place 4 - 1; no other slots appear. Used entries of a block come first, and some pair uses all 41. recv_cells[d, s, k] is -1 exactly where send_rows[s, d, k] is -1; otherwise its row is at most 14 and its column at most 126, so all four corners lie in strip d; the largest cell is reached. `recv_weight`: the four weights of an entry are the bilinear weights of a point in the donor cell and sum to one.
All inputs are finite; a program needn't handle non-finite values.
Results may differ from a plain program's by a relative error of at most 0.0049.
Values may be sent and summed in bfloat16 or wider, within the bound.
A program may use at most 128 MiB of HBM per device.

v0:
```python
import jax
import jax.numpy as jnp
from jax import lax
from jax.sharding import PartitionSpec as P


def padded_2(cells, sides, width):
    for axis, dim in sides:
        count = lax.axis_size(axis)
        head = lax.slice_in_dim(cells, 0, width, axis=dim)
        tail = lax.slice_in_dim(cells, cells.shape[dim] - width, cells.shape[dim], axis=dim)
        cells = jnp.concatenate(
            [
                lax.ppermute(tail, axis, [(i, (i + 1) % count) for i in range(count)]),
                cells,
                lax.ppermute(head, axis, [((i + 1) % count, i) for i in range(count)]),
            ],
            axis=dim,
        )
    return cells


def stencil_adjoint(grad_block, kernel):
    feat_local, tile_rows, tile_cols = grad_block.shape
    padded = jnp.pad(grad_block.astype(jnp.float32), ((0, 0), (2, 2), (2, 2)))
    summed = jnp.zeros((feat_local, tile_rows + 2, tile_cols + 2), jnp.float32)
    for row_shift in (-1, 0, 1):
        for col_shift in (-1, 0, 1):
            kernel_tap = kernel[:, 3 * (row_shift + 1) + col_shift + 1]
            window_part = padded[
                :,
                1 - row_shift : 3 - row_shift + tile_rows,
                1 - col_shift : 3 - col_shift + tile_cols,
            ]
            summed = summed + kernel_tap[:, None, None] * window_part
    return summed


def cycle_of(extended):
    return jnp.concatenate(
        [extended[:, 0, :], extended[:, -1, :], extended[:, 1:-1, 0], extended[:, 1:-1, -1]], axis=1
    )


def deposit(running, values, cell_index, weight_rows, row_length):
    is_used = cell_index >= 0
    base_cell = jnp.maximum(cell_index, 0)
    spread = values.astype(jnp.float32)
    for corner, offset in enumerate((0, 1, row_length, row_length + 1)):
        running = running.at[:, base_cell + offset].add(
            spread * jnp.where(is_used, weight_rows[corner], 0.0)[None, :]
        )
    return running


def per_device(cotangent, mix_weight, kernel, send_rows, recv_cells, recv_weight):
    feat_local, tile_rows, tile_cols = cotangent.shape
    cell_count = tile_rows * tile_cols
    flat_grad = cotangent.reshape(feat_local, cell_count)
    level_index = lax.axis_index("lev")
    own_rows = lax.dynamic_slice_in_dim(mix_weight, level_index * feat_local, feat_local, 0)
    weight_rows = lax.all_gather(own_rows, "tile", axis=1, tiled=True)
    grad_mix = jnp.dot(
        weight_rows,
        lax.all_gather(flat_grad, "lev", axis=0, tiled=True),
        preferred_element_type=jnp.float32,
    ).astype(jnp.bfloat16)
    extended = stencil_adjoint(grad_mix.reshape(feat_local, tile_rows, tile_cols), kernel)
    cycle_values = cycle_of(extended).astype(jnp.bfloat16)
    tile_count = lax.axis_size("tile")
    strip_count = tile_count // 2
    tile_here = lax.axis_index("tile")
    place_index = (tile_here + strip_count // 2) % tile_count % strip_count
    keep_top = (place_index != 0).astype(jnp.float32)
    keep_bottom = (place_index != strip_count - 1).astype(jnp.float32)
    edge_rows = jnp.stack(
        [extended[:, 0, 1:-1] * keep_top, extended[:, -1, 1:-1] * keep_bottom], axis=1
    )
    bordered = padded_2(edge_rows.astype(jnp.bfloat16), (("tile", 1),), 1).astype(edge_rows.dtype)
    interior = extended[:, 1:-1, 1:-1]
    interior = interior.at[:, 0, :].add(bordered[:, 0, :]).at[:, -1, :].add(bordered[:, 3, :])
    running = interior.reshape(feat_local, cell_count)
    cell_lists = recv_cells[0]
    weight_lists = recv_weight[0]
    slot_lists = lax.all_to_all(send_rows[0], "tile", split_axis=0, concat_axis=0, tiled=True)
    cycle_size = cycle_values.shape[1]
    shard_piece = lax.all_gather(cycle_values, "tile", axis=1, tiled=True)
    sources = shard_piece.shape[1] // cycle_size
    local_slots = (
        jnp.arange(sources, dtype=jnp.int32)[:, None] * cycle_size + jnp.maximum(slot_lists, 0)
    ).reshape(-1)
    values = jnp.take(shard_piece, local_slots, axis=1)
    cells_part = cell_lists.reshape(-1)
    weights_part = weight_lists.reshape(4, -1)
    running = deposit(running, values, cells_part, weights_part, tile_cols)
    return running.reshape(feat_local, tile_rows, tile_cols).astype(jnp.bfloat16)


def solution(mesh):
    in_specs = (
        P("lev", "tile", None),
        P(None, "tile"),
        P("lev", None),
        P("tile", None, None),
        P("tile", None, None),
        P("tile", None, None, None),
    )
    out_specs = P("lev", "tile", None)
    return jax.shard_map(
        per_device, mesh=mesh, in_specs=in_specs, out_specs=out_specs, check_vma=False
    )
```

profile of v0, /device:TPU:0, one launch (start us, length us, event | category | flops | bytes accessed | tf_op | source)
XLA Modules:
  0.0 363.0 jit_solution(4709097112009996498)
XLA Ops:
  6.5 1.7 copy-done
  8.2 0.9 constant_dynamic-slice_fusion
  9.1 4.9 %copy.22 = bf16[96,8,16,128]{3,1,2,0:T(8,128)(2,1)} copy(bf16[96,8,16,128]{3,2,1,0:T(8,128)(2,1)} %bitcast.36) | data formatting | bytes 6291456
  14.1 0.1 slice_reduce_fusion.8
  14.2 79.0 %all-gather.5.cloned.1.call-done = bf16[768,3072]{1,0:T(8,128)(2,1)} async-done(((bf16[768,384]{1,0:T(8,128)(2,1)}), bf16[768,3072]{1,0:T(8,128)(2,1)}) %all-gather.5.cloned.1.call-update) | async-done | bytes 4718608 | tf_op jit(solution)/shard_map/all_gather | solution.py:62
  93.2 81.9 %all-gather.7.cloned.1.call-done = bf16[3072,2048]{1,0:T(8,128)(2,1)} async-done(((bf16[768,2048]{1,0:T(8,128)(2,1)}), bf16[3072,2048]{1,0:T(8,128)(2,1)}) %all-gather.7.cloned.1.call-update) | async-done | bytes 12582928 | tf_op jit(solution)/shard_map/all_gather | solution.py:65
  175.0 15.4 %convolution_convert_fusion = bf16[768,2048]{1,0:T(8,128)(2,1)} fusion(bf16[768,3072]{1,0:T(8,128)(2,1)} %all-gather.5.cloned.1.call-done, bf16[3072,2048]{1,0:T(8,128)(2,1)} %all-gather.7.cloned.1.call-done), kind=kOutput, calls=%fused_computation.23 | convolution fusion | flops 9665249280 | bytes 20447232 | tf_op jit(solution)/shard_map/dot_general | solution.py:63
  190.4 4.7 %copy.15 = bf16[768,2048]{0,1:T(8,128)(2,1)} copy(bf16[768,2048]{1,0:T(8,128)(2,1)} %convolution_convert_fusion) | data formatting | bytes 6291456 | tf_op jit(solution)/shard_map/convert_element_type | solution.py:25
  195.1 5.8 %pad_convert_fusion = f32[768,20,132]{0,2,1:T(8,128)} fusion(bf16[768,16,128]{0,2,1:T(8,128)(2,1)} %bitcast.34), kind=kLoop, calls=%fused_computation.22 | loop fusion | flops 2027520 | bytes 11255808 | tf_op jit(solution)/shard_map/jit(_pad)/pad | solution.py:25
  200.9 28.3 %fusion.25 = (bf16[768,18,130]{0,2,1:T(8,128)(2,1)}, f32[768,18,130]{0,2,1:T(8,128)}) fusion(f32[768,20,132]{0,2,1:T(8,128)} %pad_convert_fusion, f32[768]{0:T(1024)S(1)} %get-tuple-element.36, f32[768]{0:T(1024)S(1)} %get-tuple-element.37, f32[768]{0:T(1024)S(1)} %get-tuple-element.30, f32[768]{0:T(1024)S(1)} %get-tuple-element.31, ...), kind=kLoop, calls=%fused_computation.90 | loop fusion | flops 32348160 | bytes 75506688 | tf_op jit(solution)/shard_map/convert.14
  229.2 1.1 fusion.27
  230.3 1.1 slice_bitcast_fusion.1
  231.4 0.8 maximum_bitcast_fusion
  232.3 5.5 %all-to-all-start = ((s32[8,1,41]{2,1,0:T(1,128)}), s32[8,1,41]{2,1,0:T(1,128)S(1)}, u32[]{:S(2)}, u32[]{:S(2)}) async-start(s32[8,1,41]{2,1,0:T(1,128)} %bitcast.2), calls=%async_computation | async-start | bytes 8192 | tf_op jit(solution)/shard_map/all_to_all | solution.py:85
  237.8 0.1 squeeze.37
  237.9 0.1 squeeze.38
  238.0 0.1 squeeze.39
  238.0 0.1 squeeze.40
  238.1 0.1 ge.30
  238.2 0.1 reshape.278
  238.3 0.1 reshape.280
  238.4 0.1 reshape.282
  238.5 0.1 reshape.284
  238.6 0.1 reshape.286
  238.6 0.1 reshape.288
  238.8 0.1 add.204
  238.9 0.1 add.209
  239.0 0.1 add.205
  239.1 0.1 reshape.246
  239.2 5.0 %all-to-all-done = s32[8,1,41]{2,1,0:T(1,128)S(1)} async-done(((s32[8,1,41]{2,1,0:T(1,128)}), s32[8,1,41]{2,1,0:T(1,128)S(1)}, u32[]{:S(2)}, u32[]{:S(2)}) %all-to-all-start) | async-done | bytes 1344 | tf_op jit(solution)/shard_map/all_to_all | solution.py:85
  244.2 0.1 max.55
  244.3 0.1 max.53
  244.4 1.2 fusion.19
  245.6 0.6 collective-permute-start
  246.2 4.2 %collective-permute-start.1 = (bf16[768,1,128]{0,2,1:T(8,128)(2,1)S(1)}, bf16[768,1,128]{0,2,1:T(8,128)(2,1)S(1)}, u32[]{:S(2)}, u32[]{:S(2)}) collective-permute-start(bf16[768,1,128]{0,2,1:T(8,128)(2,1)S(1)} %get-tuple-element.41), channel_id=1, source_target_pairs={{4,0},{8,4},{12,8},{16,12},{20,16},{24,20},{28,24},{0,28},{5,1},{9... | collective-permute-start | bytes 589832 | tf_op jit(solution)/shard_map/ppermute | solution.py:16
  250.4 6.3 %slice.198 = f32[768,16,128]{0,2,1:T(8,128)} slice(f32[768,18,130]{0,2,1:T(8,128)} %get-tuple-element.39), slice={[0:768], [1:17], [1:129]} | slice | bytes 12582912 | tf_op jit(solution)/shard_map/slice | solution.py:80
  256.7 2.9 collective-permute-done
  259.6 1.8 fusion.17
  261.4 1.8 fusion.16
  263.2 40.2 %all-gather.9.cloned.1.call-done = bf16[8,292,768]{2,1,0:T(8,128)(2,1)} async-done(((bf16[1,292,768]{2,1,0:T(8,128)(2,1)}), bf16[8,292,768]{2,1,0:T(8,128)(2,1)}) %all-gather.9.cloned.1.call-update) | async-done | bytes 3588112 | tf_op jit(solution)/shard_map/all_gather | solution.py:87
  303.4 4.7 %reshape.290 = bf16[2336,768]{1,0:T(8,128)(2,1)} reshape(bf16[8,292,768]{2,1,0:T(8,128)(2,1)} %all-gather.9.cloned.1.call-done) | data formatting | bytes 7176192
  308.1 5.0 %gather_fusion = bf16[328,768]{1,0:T(8,128)(2,1)S(1)} fusion(bf16[768,2336]{0,1:T(8,128)(2,1)} %bitcast.32, s32[1024]{0:T(1024)S(1)} %pad_clamp_fusion), kind=kCustom, calls=%fused_computation | custom fusion | bytes 1008928 | tf_op jit(solution)/shard_map/jit(_take)/gather | solution.py:92
  313.1 8.4 %scatter_custom_fusion = f32[768,2048]{0,1:T(8,128)} fusion(f32[768,2048]{0,1:T(8,128)} %bitcast.1, s32[328]{0:T(512)S(1)} %reshape.246, f32[328]{0:T(512)S(1)} %get-tuple-element.62, bf16[328,768]{1,0:T(8,128)(2,1)S(1)} %gather_fusion, pred[328]{0:T(512)(128)(4,1)S(1)} %compare_and_fusion), kind=kCustom, calls=%fused_computation.30 | custom fusion | flops 1007616 | bytes 6797824 | tf_op jit(solution)/shard_map/scatter-add | solution.py:50
  321.4 8.4 %scatter_custom_fusion.1 = f32[768,2048]{0,1:T(8,128)} fusion(f32[768,2048]{0,1:T(8,128)} %scatter_custom_fusion, s32[328]{0:T(512)S(1)} %fusion.21, f32[328]{0:T(512)S(1)} %get-tuple-element.61, bf16[328,768]{1,0:T(8,128)(2,1)S(1)} %gather_fusion, pred[328]{0:T(512)(128)(4,1)S(1)} %compare_and_fusion), kind=kCustom, calls=%fused_computation.31 | custom fusion | flops 1007616 | bytes 6797824 | tf_op jit(solution)/shard_map/scatter-add | solution.py:50
  329.8 8.4 %scatter_custom_fusion.2 = f32[768,2048]{0,1:T(8,128)} fusion(f32[768,2048]{0,1:T(8,128)} %scatter_custom_fusion.1, s32[328]{0:T(512)S(1)} %fusion.22, f32[328]{0:T(512)S(1)} %get-tuple-element.60, bf16[328,768]{1,0:T(8,128)(2,1)S(1)} %gather_fusion, pred[328]{0:T(512)(128)(4,1)S(1)} %compare_and_fusion), kind=kCustom, calls=%fused_computation.32 | custom fusion | flops 1007616 | bytes 6797824 | tf_op jit(solution)/shard_map/scatter-add | solution.py:50
  338.2 8.5 %scatter_custom_fusion.3 = f32[768,2048]{0,1:T(8,128)} fusion(f32[768,2048]{0,1:T(8,128)} %scatter_custom_fusion.2, s32[328]{0:T(512)S(1)} %fusion.23, f32[328]{0:T(512)S(1)} %get-tuple-element.59, bf16[328,768]{1,0:T(8,128)(2,1)S(1)} %gather_fusion, pred[328]{0:T(512)(128)(4,1)S(1)} %compare_and_fusion), kind=kCustom, calls=%fused_computation.29 | custom fusion | flops 1007616 | bytes 6797824 | tf_op jit(solution)/shard_map/scatter-add | solution.py:50
  346.7 4.8 %convert_element_type.35 = bf16[768,2048]{0,1:T(8,128)(2,1)} convert(f32[768,2048]{0,1:T(8,128)} %scatter_custom_fusion.3) | non-fusion elementwise | flops 1572864 | bytes 9437184 | tf_op jit(solution)/shard_map/convert_element_type | solution.py:96
  351.5 5.0 %copy.14 = bf16[768,16,128]{2,1,0:T(8,128)(2,1)} copy(bf16[768,16,128]{0,2,1:T(8,128)(2,1)} %bitcast.35) | data formatting | bytes 6291456 | tf_op jit(solution)/shard_map/convert_element_type | solution.py:96
  (29 shorter events, 0.3 us)
Async XLA Ops:
  6.5 1.7 copy-start
  6.5 7.5 %copy-start.4 = (f32[768,9]{0,1:T(8,128)S(1)}, f32[768,9]{0,1:T(8,128)}, u32[]{:S(2)}) copy-start(f32[768,9]{0,1:T(8,128)} %param.12) | copy-start | bytes 82948
  6.5 86.6 %all-gather.5.cloned.1.call-start = ((), (), s32[]{:S(2)}) async-start(), calls=%async_computation.1 | async-start | bytes 5308416 | tf_op jit(solution)/shard_map/all_gather | solution.py:62
  9.1 165.9 %all-gather.7.cloned.1.call-start = ((), (), s32[]{:S(2)}) async-start(), calls=%async_computation.2 | async-start | bytes 15728640 | tf_op jit(solution)/shard_map/all_gather | solution.py:65
  14.0 289.4 %all-gather.9.cloned.1.call-start = ((), (), s32[]{:S(2)}) async-start(), calls=%async_computation.3 | async-start | bytes 4091904 | tf_op jit(solution)/shard_map/all_gather | solution.py:87
  200.9 36.8 %copy-start.2 = (f32[1,4,8,41]{3,2,1,0:T(8,128)S(1)}, f32[1,4,8,41]{3,2,1,0:T(8,128)}, u32[]{:S(2)}) copy-start(f32[1,4,8,41]{3,2,1,0:T(8,128)} %param.15) | copy-start | bytes 15748
  200.9 37.2 %copy-start.3 = (s32[1,8,41]{2,1,0:T(8,128)S(1)}, s32[1,8,41]{2,1,0:T(8,128)}, u32[]{:S(2)}) copy-start(s32[1,8,41]{2,1,0:T(8,128)} %param.14) | copy-start | bytes 3940
  232.3 11.9 %all-to-all-start = ((s32[8,1,41]{2,1,0:T(1,128)}), s32[8,1,41]{2,1,0:T(1,128)S(1)}, u32[]{:S(2)}, u32[]{:S(2)}) async-start(s32[8,1,41]{2,1,0:T(1,128)} %bitcast.2), calls=%async_computation | async-start | bytes 8192 | tf_op jit(solution)/shard_map/all_to_all | solution.py:85
  245.6 14.0 %collective-permute-start = (bf16[768,1,128]{0,2,1:T(8,128)(2,1)S(1)}, bf16[768,1,128]{0,2,1:T(8,128)(2,1)S(1)}, u32[]{:S(2)}, u32[]{:S(2)}) collective-permute-start(bf16[768,1,128]{0,2,1:T(8,128)(2,1)S(1)} %get-tuple-element.40), channel_id=1, source_target_pairs={{0,4},{4,8},{8,12},{12,16},{16,20},{20,24},{24,28},{28,0},{1,5},{5... | collective-permute-start | bytes 589832 | tf_op jit(solution)/shard_map/ppermute | solution.py:14
  246.2 13.4 %collective-permute-start.1 = (bf16[768,1,128]{0,2,1:T(8,128)(2,1)S(1)}, bf16[768,1,128]{0,2,1:T(8,128)(2,1)S(1)}, u32[]{:S(2)}, u32[]{:S(2)}) collective-permute-start(bf16[768,1,128]{0,2,1:T(8,128)(2,1)S(1)} %get-tuple-element.41), channel_id=1, source_target_pairs={{4,0},{8,4},{12,8},{16,12},{20,16},{24,20},{28,24},{0,28},{5,1},{9... | collective-permute-start | bytes 589832 | tf_op jit(solution)/shard_map/ppermute | solution.py:16
  338.2 18.3 %copy-start.1 = (bf16[3072,384]{1,0:T(8,128)(2,1)S(1)}, bf16[3072,384]{1,0:T(8,128)(2,1)}, u32[]{:S(2)}) copy-start(bf16[3072,384]{1,0:T(8,128)(2,1)} %param.11) | copy-start | bytes 7077892
Sparse Core Ops, SparseCore 0:
  9.4 83.6 all-gather.4
  94.7 80.2 all-gather.6
  232.4 70.9 all-gather.8
where the time goes:
time: 364 us; the launch traced here: 363 us
  waiting for transfers between devices  209 us (57%)
  other arithmetic  78.3 us (22%)
  local copies, waits for them, and re-layouts  36.6 us (10%)
  matrix products  15.4 us (4%)
  between operations  13.3 us (4%)
  starting transfers between devices  10.4 us (3%)
    all_gather x1, waiting for transfers between devices, per_device(): lax.all_gather(flat_grad, 'lev', axis=0, tiled=True)  81.9 us
    all_gather x1, waiting for transfers between devices, per_device(): weight_rows = lax.all_gather(own_rows, 'tile', axis=1, tiled=True)  79 us
    all_gather x1, waiting for transfers between devices, per_device(): shard_piece = lax.all_gather(cycle_values, 'tile', axis=1, tiled=True)  40.2 us
    scatter-add x4, other arithmetic, deposit(): running.at[:, base_cell + offset]  33.6 us
    another operation x1, other arithmetic  28.3 us
    dot_general x1, matrix products, per_device(): jnp.dot(weight_rows, lax.all_gather(flat_grad, 'lev', axis=0, tiled=True)...  15.4 us
    unnamed x13, local copies, waits for them, and re-layouts  11.3 us
  transfers between devices with their start and end apart: 6, of which 5 were waited for; matrix products, arithmetic and copies ran while one was open for 5% of the time, Pallas kernels for 0%

commit v1 on v0

--- a/solution.py
+++ b/solution.py
@@ -2,6 +2,28 @@
 import jax.numpy as jnp
 from jax import lax
 from jax.sharding import PartitionSpec as P
+
+
+def laid_out(blocks, dim):
+    blocks = jnp.moveaxis(blocks, 0, dim)
+    lengths = blocks.shape
+    return blocks.reshape(*lengths[:dim], lengths[dim] * lengths[dim + 1], *lengths[dim + 2 :])
+
+
+def gather_around(array, axis, dim):
+    size = lax.axis_size(axis)
+    pairs = [(i, (i + 1) % size) for i in range(size)]
+    back = [(b, a) for a, b in pairs]
+    lower, upper = ([], [])
+    for step in range(size - 1):
+        if step % 2 == 0:
+            lower.append(lax.ppermute(lower[-1] if lower else array, axis, pairs))
+        else:
+            upper.append(lax.ppermute(upper[-1] if upper else array, axis, back))
+    parts = jnp.stack([*lower[::-1], array, *upper])
+    shift = lax.axis_index(axis) - len(lower)
+    parts = parts[(jnp.arange(size) - shift) % size]
+    return laid_out(parts, dim)
 
 
 def padded_2(cells, sides, width):
@@ -84,7 +106,7 @@
     weight_lists = recv_weight[0]
     slot_lists = lax.all_to_all(send_rows[0], "tile", split_axis=0, concat_axis=0, tiled=True)
     cycle_size = cycle_values.shape[1]
-    shard_piece = lax.all_gather(cycle_values, "tile", axis=1, tiled=True)
+    shard_piece = gather_around(cycle_values, "tile", 1)
     sources = shard_piece.shape[1] // cycle_size
     local_slots = (
         jnp.arange(sources, dtype=jnp.int32)[:, None] * cycle_size + jnp.maximum(slot_lists, 0)

time: 364 us -> 386 us (1.060)
  starting transfers between devices: 10.4 us -> 26.3 us
  local copies, waits for them, and re-layouts: 36.6 us -> 47.2 us
  waiting for transfers between devices: 209 us -> 205 us
    ppermute x0 -> x7, waiting for transfers between devices: none -> 50.7 us  [the longest x4 37.4 us: gather_around(): lower.append(lax.ppermute(lower[-1] if lower else array, axis, pairs))]
    all_gather x1 -> x0, waiting for transfers between devices: 40.2 us -> none  [per_device(): shard_piece = lax.all_gather(cycle_values, 'tile', axis=1, tiled=True)]
    another operation x1 -> x0, other arithmetic: 28.3 us -> none
    add x0 -> x1, other arithmetic: none -> 26.9 us  [stencil_adjoint(): summed = summed + kernel_tap[:, None, None] * window_part]
    ppermute x0 -> x7, starting transfers between devices: none -> 16.6 us  [the longest x3 10.1 us: gather_around(): upper.append(lax.ppermute(upper[-1] if upper else array, axis, back))]
    all_gather x1, waiting for transfers between devices: 79 us -> 70.8 us  [per_device(): weight_rows = lax.all_gather(own_rows, 'tile', axis=1, tiled=True)]
    all_to_all x1, waiting for transfers between devices: 5.02 us -> 0.01 us  [per_device(): lax.all_to_all(send_rows[0], 'tile', split_axis=0, concat_axis=0, tiled=T...]
    reshape x0 -> x1, local copies, waits for them, and re-layouts: none -> 4.71 us  [laid_out(): blocks.reshape(*lengths[:dim], lengths[dim] * lengths[dim + 1], *lengths[...]
  transfers between devices with their start and end apart: 6 -> 12, of which waited for: 5 -> 8; matrix products, arithmetic and copies ran while one was open for 5% -> 20% of each run, Pallas kernels for 0% -> 0%
where the time goes in v1:
time: 386 us; the launch traced here: 385 us
  waiting for transfers between devices  205 us (53%)
  other arithmetic  77 us (20%)
  local copies, waits for them, and re-layouts  47.2 us (12%)
  starting transfers between devices  26.3 us (7%)
  matrix products  15.4 us (4%)
  between operations  13.6 us (4%)
    all_gather x1, waiting for transfers between devices, per_device(): lax.all_gather(flat_grad, 'lev', axis=0, tiled=True)  81.9 us
    all_gather x1, waiting for transfers between devices, per_device(): weight_rows = lax.all_gather(own_rows, 'tile', axis=1, tiled=True)  70.8 us
    ppermute x4, waiting for transfers between devices, gather_around(): lower.append(lax.ppermute(lower[-1] if lower else array, axis, pairs))  37.4 us
    scatter-add x4, other arithmetic, deposit(): running.at[:, base_cell + offset]  33.6 us
    add x1, other arithmetic, stencil_adjoint(): summed = summed + kernel_tap[:, None, None] * window_part  26.9 us
    dot_general x1, matrix products, per_device(): jnp.dot(weight_rows, lax.all_gather(flat_grad, 'lev', axis=0, tiled=True)...  15.4 us
    ppermute x3, waiting for transfers between devices, gather_around(): upper.append(lax.ppermute(upper[-1] if upper else array, axis, back))  13.3 us
    unnamed x18, local copies, waits for them, and re-layouts  11.4 us
  transfers between devices with their start and end apart: 12, of which 8 were waited for; matrix products, arithmetic and copies ran while one was open for 20% of the time, Pallas kernels for 0%

profile of v1, /device:TPU:0, one launch (start us, length us, event | category | flops | bytes accessed | tf_op | source)
XLA Modules:
  0.0 384.6 jit_solution(13841306222062664544)
XLA Ops:
  6.6 1.6 copy-done
  8.2 0.9 constant_dynamic-slice_fusion
  9.1 4.9 %copy.26 = bf16[96,8,16,128]{3,1,2,0:T(8,128)(2,1)} copy(bf16[96,8,16,128]{3,2,1,0:T(8,128)(2,1)} %bitcast.58) | data formatting | bytes 6291456
  14.0 7.3 %all-to-all-start = ((s32[8,1,41]{2,1,0:T(1,128)}), s32[8,1,41]{2,1,0:T(1,128)S(1)}, u32[]{:S(2)}, u32[]{:S(2)}) async-start(s32[8,1,41]{2,1,0:T(1,128)} %bitcast.2), calls=%async_computation | async-start | bytes 8192 | tf_op jit(solution)/shard_map/all_to_all | solution.py:107
  21.3 0.1 ge.30
  22.1 0.1 reshape.412
  22.4 70.8 %all-gather.3.cloned.1.call-done = bf16[768,3072]{1,0:T(8,128)(2,1)} async-done(((bf16[768,384]{1,0:T(8,128)(2,1)}), bf16[768,3072]{1,0:T(8,128)(2,1)}) %all-gather.3.cloned.1.call-update) | async-done | bytes 4718608 | tf_op jit(solution)/shard_map/all_gather | solution.py:84
  93.2 81.9 %all-gather.5.cloned.1.call-done = bf16[3072,2048]{1,0:T(8,128)(2,1)} async-done(((bf16[768,2048]{1,0:T(8,128)(2,1)}), bf16[3072,2048]{1,0:T(8,128)(2,1)}) %all-gather.5.cloned.1.call-update) | async-done | bytes 12582928 | tf_op jit(solution)/shard_map/all_gather | solution.py:87
  175.1 15.4 %convolution_convert_fusion = bf16[768,2048]{1,0:T(8,128)(2,1)} fusion(bf16[768,3072]{1,0:T(8,128)(2,1)} %all-gather.3.cloned.1.call-done, bf16[3072,2048]{1,0:T(8,128)(2,1)} %all-gather.5.cloned.1.call-done), kind=kOutput, calls=%fused_computation.24 | convolution fusion | flops 9665249280 | bytes 20447232 | tf_op jit(solution)/shard_map/dot_general | solution.py:85
  190.5 4.7 %copy.15 = bf16[768,2048]{0,1:T(8,128)(2,1)} copy(bf16[768,2048]{1,0:T(8,128)(2,1)} %convolution_convert_fusion) | data formatting | bytes 6291456 | tf_op jit(solution)/shard_map/convert_element_type | solution.py:47
  195.2 5.8 %pad_convert_fusion = f32[768,20,132]{0,2,1:T(8,128)} fusion(bf16[768,16,128]{0,2,1:T(8,128)(2,1)} %bitcast.56), kind=kLoop, calls=%fused_computation.23 | loop fusion | flops 2027520 | bytes 11255808 | tf_op jit(solution)/shard_map/jit(_pad)/pad | solution.py:47
  201.0 26.9 %fusion = f32[768,18,130]{0,2,1:T(8,128)} fusion(f32[768,20,132]{0,2,1:T(8,128)} %pad_convert_fusion, f32[768]{0:T(1024)S(1)} %get-tuple-element.36, f32[768]{0:T(1024)S(1)} %get-tuple-element.37, f32[768]{0:T(1024)S(1)} %get-tuple-element.30, f32[768]{0:T(1024)S(1)} %get-tuple-element.31, f32[768]{0:T(1024)S(1)} %get-tuple-element.32, ...), kind=kLoop, calls=%fused_computation.7 | loop fusion | flops 30551040 | bytes 71912448 | tf_op jit(solution)/shard_map/add | solution.py:57
  227.9 1.2 fusion.31
  229.1 1.2 fusion.20
  230.4 1.5 collective-permute-start.2
  232.1 0.1 add.235
  232.3 13.5 %collective-permute-done.2 = bf16[768,292]{0,1:T(8,128)(2,1)S(1)} collective-permute-done((bf16[768,292]{0,1:T(8,128)(2,1)S(1)}, bf16[768,292]{0,1:T(8,128)(2,1)S(1)}, u32[]{:S(2)}, u32[]{:S(2)}) %collective-permute-start.2) | collective-permute-done | bytes 448544 | tf_op jit(solution)/shard_map/ppermute | solution.py:20
  246.0 4.8 %collective-permute-start.6 = (bf16[768,292]{0,1:T(8,128)(2,1)S(1)}, bf16[768,292]{0,1:T(8,128)(2,1)S(1)}, u32[]{:S(2)}, u32[]{:S(2)}) collective-permute-start(bf16[768,292]{0,1:T(8,128)(2,1)S(1)} %pad_maximum_fusion), channel_id=1, source_target_pairs={{4,0},{8,4},{12,8},{16,12},{20,16},{24,20},{28,24},{0,28},{5,1},{9... | collective-permute-start | bytes 1345544 | tf_op jit(solution)/shard_map/ppermute | solution.py:22
  250.8 14.3 %collective-permute-done.3 = bf16[768,292]{0,1:T(8,128)(2,1)S(1)} collective-permute-done((bf16[768,292]{0,1:T(8,128)(2,1)S(1)}, bf16[768,292]{0,1:T(8,128)(2,1)S(1)}, u32[]{:S(2)}, u32[]{:S(2)}) %collective-permute-start.3) | collective-permute-done | bytes 448544 | tf_op jit(solution)/shard_map/ppermute | solution.py:20
  265.1 2.5 collective-permute-start.4
  267.6 1.2 fusion.19
  268.8 2.3 collective-permute-start.1
  271.1 6.3 %slice.196 = f32[768,16,128]{0,2,1:T(8,128)} slice(f32[768,18,130]{0,2,1:T(8,128)} %fusion), slice={[0:768], [1:17], [1:129]} | slice | bytes 12582912 | tf_op jit(solution)/shard_map/slice | solution.py:102
  277.4 5.4 %collective-permute-start.7 = (bf16[768,292]{0,1:T(8,128)(2,1)S(1)}, bf16[768,292]{0,1:T(8,128)(2,1)S(1)}, u32[]{:S(2)}, u32[]{:S(2)}) collective-permute-start(bf16[768,292]{0,1:T(8,128)(2,1)S(1)} %collective-permute-done.6), channel_id=1, source_target_pairs={{4,0},{8,4},{12,8},{16,12},{20,16},{24,20},{28,24},{0,28},{5,1},{9... | collective-permute-start | bytes 1345544 | tf_op jit(solution)/shard_map/ppermute | solution.py:22
  282.7 9.7 %collective-permute-done.4 = bf16[768,292]{0,1:T(8,128)(2,1)S(1)} collective-permute-done((bf16[768,292]{0,1:T(8,128)(2,1)S(1)}, bf16[768,292]{0,1:T(8,128)(2,1)S(1)}, u32[]{:S(2)}, u32[]{:S(2)}) %collective-permute-start.4) | collective-permute-done | bytes 448544 | tf_op jit(solution)/shard_map/ppermute | solution.py:20
  292.4 2.5 collective-permute-start.5
  294.9 1.7 collective-permute-done
  296.6 1.8 fusion.17
  298.4 1.8 fusion.16
  300.2 6.7 %collective-permute-done.7 = bf16[768,292]{0,1:T(8,128)(2,1)S(1)} collective-permute-done((bf16[768,292]{0,1:T(8,128)(2,1)S(1)}, bf16[768,292]{0,1:T(8,128)(2,1)S(1)}, u32[]{:S(2)}, u32[]{:S(2)}) %collective-permute-start.7) | collective-permute-done | bytes 448544 | tf_op jit(solution)/shard_map/ppermute | solution.py:22
  306.9 0.8 bitcast_dynamic-update-slice_fusion.6
  307.7 0.8 bitcast_dynamic-update-slice_fusion.5
  308.5 0.8 bitcast_dynamic-update-slice_fusion.4
  309.3 0.8 bitcast_dynamic-update-slice_fusion.3
  310.1 0.8 maximum_dynamic-update-slice_fusion
  311.0 0.8 bitcast_dynamic-update-slice_fusion.2
  311.7 0.8 bitcast_dynamic-update-slice_fusion.1
  312.6 6.6 %collective-permute-done.8 = bf16[768,292]{0,1:T(8,128)(2,1)S(1)} collective-permute-done((bf16[768,292]{0,1:T(8,128)(2,1)S(1)}, bf16[768,292]{0,1:T(8,128)(2,1)S(1)}, u32[]{:S(2)}, u32[]{:S(2)}) %collective-permute-start.8) | collective-permute-done | bytes 448544 | tf_op jit(solution)/shard_map/ppermute | solution.py:22
  319.2 0.8 bitcast_dynamic-update-slice_fusion
  320.1 4.7 %gather_fusion = bf16[8,768,292]{1,2,0:T(8,128)(2,1)} fusion(bf16[8,768,292]{1,2,0:T(8,128)(2,1)} %bitcast_dynamic-update-slice_fusion, s32[1024]{0:T(1024)S(1)} %pad_clamp_fusion.1), kind=kCustom, calls=%fused_computation | custom fusion | bytes 7176224 | tf_op jit(solution)/shard_map/gather | solution.py:25
  324.7 4.7 %reshape.351 = bf16[768,2336]{0,1:T(8,128)(2,1)} reshape(bf16[768,8,292]{0,2,1:T(8,128)(2,1)} %bitcast.54) | data formatting | bytes 7176192 | tf_op jit(solution)/shard_map/reshape | solution.py:10
  329.4 5.0 %gather_fusion.1 = bf16[328,768]{1,0:T(8,128)(2,1)S(1)} fusion(bf16[768,2336]{0,1:T(8,128)(2,1)} %reshape.351, s32[1024]{0:T(1024)S(1)} %pad_clamp_fusion), kind=kCustom, calls=%fused_computation.1 | custom fusion | bytes 1008928 | tf_op jit(solution)/shard_map/jit(_take)/gather | solution.py:114
  334.4 8.4 %scatter_custom_fusion = f32[768,2048]{0,1:T(8,128)} fusion(f32[768,2048]{0,1:T(8,128)} %bitcast.1, s32[328]{0:T(512)S(1)} %reshape.370, f32[328]{0:T(512)S(1)} %get-tuple-element.66, bf16[328,768]{1,0:T(8,128)(2,1)S(1)} %gather_fusion.1, pred[328]{0:T(512)(128)(4,1)S(1)} %compare_and_fusion), kind=kCustom, calls=%fused_computation.31 | custom fusion | flops 1007616 | bytes 6797824 | tf_op jit(solution)/shard_map/scatter-add | solution.py:72
  342.8 8.4 %scatter_custom_fusion.1 = f32[768,2048]{0,1:T(8,128)} fusion(f32[768,2048]{0,1:T(8,128)} %scatter_custom_fusion, s32[328]{0:T(512)S(1)} %fusion.25, f32[328]{0:T(512)S(1)} %get-tuple-element.65, bf16[328,768]{1,0:T(8,128)(2,1)S(1)} %gather_fusion.1, pred[328]{0:T(512)(128)(4,1)S(1)} %compare_and_fusion), kind=kCustom, calls=%fused_computation.32 | custom fusion | flops 1007616 | bytes 6797824 | tf_op jit(solution)/shard_map/scatter-add | solution.py:72
  351.1 8.4 %scatter_custom_fusion.2 = f32[768,2048]{0,1:T(8,128)} fusion(f32[768,2048]{0,1:T(8,128)} %scatter_custom_fusion.1, s32[328]{0:T(512)S(1)} %fusion.26, f32[328]{0:T(512)S(1)} %get-tuple-element.64, bf16[328,768]{1,0:T(8,128)(2,1)S(1)} %gather_fusion.1, pred[328]{0:T(512)(128)(4,1)S(1)} %compare_and_fusion), kind=kCustom, calls=%fused_computation.33 | custom fusion | flops 1007616 | bytes 6797824 | tf_op jit(solution)/shard_map/scatter-add | solution.py:72
  359.5 8.5 %scatter_custom_fusion.3 = f32[768,2048]{0,1:T(8,128)} fusion(f32[768,2048]{0,1:T(8,128)} %scatter_custom_fusion.2, s32[328]{0:T(512)S(1)} %fusion.27, f32[328]{0:T(512)S(1)} %get-tuple-element.63, bf16[328,768]{1,0:T(8,128)(2,1)S(1)} %gather_fusion.1, pred[328]{0:T(512)(128)(4,1)S(1)} %compare_and_fusion), kind=kCustom, calls=%fused_computation.30 | custom fusion | flops 1007616 | bytes 6797824 | tf_op jit(solution)/shard_map/scatter-add | solution.py:72
  368.0 4.8 %convert_element_type.42 = bf16[768,2048]{0,1:T(8,128)(2,1)} convert(f32[768,2048]{0,1:T(8,128)} %scatter_custom_fusion.3) | non-fusion elementwise | flops 1572864 | bytes 9437184 | tf_op jit(solution)/shard_map/convert_element_type | solution.py:118
  372.8 5.0 %copy.14 = bf16[768,16,128]{2,1,0:T(8,128)(2,1)} copy(bf16[768,16,128]{0,2,1:T(8,128)(2,1)} %bitcast.57) | data formatting | bytes 6291456 | tf_op jit(solution)/shard_map/convert_element_type | solution.py:118
  (51 shorter events, 1.6 us)
Async XLA Ops:
  6.5 1.7 copy-start
  6.5 14.8 %copy-start.3 = (s32[1,8,41]{2,1,0:T(8,128)S(1)}, s32[1,8,41]{2,1,0:T(8,128)}, u32[]{:S(2)}) copy-start(s32[1,8,41]{2,1,0:T(8,128)} %param.14) | copy-start | bytes 3940
  6.5 14.9 %copy-start.2 = (f32[1,4,8,41]{3,2,1,0:T(8,128)S(1)}, f32[1,4,8,41]{3,2,1,0:T(8,128)}, u32[]{:S(2)}) copy-start(f32[1,4,8,41]{3,2,1,0:T(8,128)} %param.15) | copy-start | bytes 15748
  6.5 15.8 %copy-start.4 = (f32[768,9]{0,1:T(8,128)S(1)}, f32[768,9]{0,1:T(8,128)}, u32[]{:S(2)}) copy-start(f32[768,9]{0,1:T(8,128)} %param.12) | copy-start | bytes 82948
  6.5 86.7 %all-gather.3.cloned.1.call-start = ((), (), s32[]{:S(2)}) async-start(), calls=%async_computation.1 | async-start | bytes 5308416 | tf_op jit(solution)/shard_map/all_gather | solution.py:84
  9.1 166.0 %all-gather.5.cloned.1.call-start = ((), (), s32[]{:S(2)}) async-start(), calls=%async_computation.2 | async-start | bytes 15728640 | tf_op jit(solution)/shard_map/all_gather | solution.py:87
  14.0 231.7 %all-to-all-start = ((s32[8,1,41]{2,1,0:T(1,128)}), s32[8,1,41]{2,1,0:T(1,128)S(1)}, u32[]{:S(2)}, u32[]{:S(2)}) async-start(s32[8,1,41]{2,1,0:T(1,128)} %bitcast.2), calls=%async_computation | async-start | bytes 8192 | tf_op jit(solution)/shard_map/all_to_all | solution.py:107
  230.4 15.3 %collective-permute-start.2 = (bf16[768,292]{0,1:T(8,128)(2,1)S(1)}, bf16[768,292]{0,1:T(8,128)(2,1)S(1)}, u32[]{:S(2)}, u32[]{:S(2)}) collective-permute-start(bf16[768,292]{0,1:T(8,128)(2,1)S(1)} %pad_maximum_fusion), channel_id=1, source_target_pairs={{0,4},{4,8},{8,12},{12,16},{16,20},{20,24},{24,28},{28,0},{1,5},{5... | collective-permute-start | bytes 1345544 | tf_op jit(solution)/shard_map/ppermute | solution.py:20
  245.8 19.3 %collective-permute-start.3 = (bf16[768,292]{0,1:T(8,128)(2,1)S(1)}, bf16[768,292]{0,1:T(8,128)(2,1)S(1)}, u32[]{:S(2)}, u32[]{:S(2)}) collective-permute-start(bf16[768,292]{0,1:T(8,128)(2,1)S(1)} %collective-permute-done.2), channel_id=1, source_target_pairs={{0,4},{4,8},{8,12},{12,16},{16,20},{20,24},{24,28},{28,0},{1,5},{5... | collective-permute-start | bytes 1345544 | tf_op jit(solution)/shard_map/ppermute | solution.py:20
  246.0 31.4 %collective-permute-start.6 = (bf16[768,292]{0,1:T(8,128)(2,1)S(1)}, bf16[768,292]{0,1:T(8,128)(2,1)S(1)}, u32[]{:S(2)}, u32[]{:S(2)}) collective-permute-start(bf16[768,292]{0,1:T(8,128)(2,1)S(1)} %pad_maximum_fusion), channel_id=1, source_target_pairs={{4,0},{8,4},{12,8},{16,12},{20,16},{24,20},{28,24},{0,28},{5,1},{9... | collective-permute-start | bytes 1345544 | tf_op jit(solution)/shard_map/ppermute | solution.py:22
  265.1 27.3 %collective-permute-start.4 = (bf16[768,292]{0,1:T(8,128)(2,1)S(1)}, bf16[768,292]{0,1:T(8,128)(2,1)S(1)}, u32[]{:S(2)}, u32[]{:S(2)}) collective-permute-start(bf16[768,292]{0,1:T(8,128)(2,1)S(1)} %collective-permute-done.3), channel_id=1, source_target_pairs={{0,4},{4,8},{8,12},{12,16},{16,20},{20,24},{24,28},{28,0},{1,5},{5... | collective-permute-start | bytes 1345544 | tf_op jit(solution)/shard_map/ppermute | solution.py:20
  268.8 26.1 %collective-permute-start.1 = (bf16[768,1,128]{0,2,1:T(8,128)(2,1)S(1)}, bf16[768,1,128]{0,2,1:T(8,128)(2,1)S(1)}, u32[]{:S(2)}, u32[]{:S(2)}) collective-permute-start(bf16[768,1,128]{0,2,1:T(8,128)(2,1)S(1)} %get-tuple-element.45), channel_id=1, source_target_pairs={{4,0},{8,4},{12,8},{16,12},{20,16},{24,20},{28,24},{0,28},{5,1},{9... | collective-permute-start | bytes 589832 | tf_op jit(solution)/shard_map/ppermute | solution.py:38
  271.1 25.5 %collective-permute-start = (bf16[768,1,128]{0,2,1:T(8,128)(2,1)S(1)}, bf16[768,1,128]{0,2,1:T(8,128)(2,1)S(1)}, u32[]{:S(2)}, u32[]{:S(2)}) collective-permute-start(bf16[768,1,128]{0,2,1:T(8,128)(2,1)S(1)} %get-tuple-element.44), channel_id=1, source_target_pairs={{0,4},{4,8},{8,12},{12,16},{16,20},{20,24},{24,28},{28,0},{1,5},{5... | collective-permute-start | bytes 589832 | tf_op jit(solution)/shard_map/ppermute | solution.py:36
  277.4 29.5 %collective-permute-start.7 = (bf16[768,292]{0,1:T(8,128)(2,1)S(1)}, bf16[768,292]{0,1:T(8,128)(2,1)S(1)}, u32[]{:S(2)}, u32[]{:S(2)}) collective-permute-start(bf16[768,292]{0,1:T(8,128)(2,1)S(1)} %collective-permute-done.6), channel_id=1, source_target_pairs={{4,0},{8,4},{12,8},{16,12},{20,16},{24,20},{28,24},{0,28},{5,1},{9... | collective-permute-start | bytes 1345544 | tf_op jit(solution)/shard_map/ppermute | solution.py:22
  292.4 14.5 %collective-permute-start.5 = (bf16[768,292]{0,1:T(8,128)(2,1)S(1)}, bf16[768,292]{0,1:T(8,128)(2,1)S(1)}, u32[]{:S(2)}, u32[]{:S(2)}) collective-permute-start(bf16[768,292]{0,1:T(8,128)(2,1)S(1)} %collective-permute-done.4), channel_id=1, source_target_pairs={{0,4},{4,8},{8,12},{12,16},{16,20},{20,24},{24,28},{28,0},{1,5},{5... | collective-permute-start | bytes 1345544 | tf_op jit(solution)/shard_map/ppermute | solution.py:20
  306.9 12.4 %collective-permute-start.8 = (bf16[768,292]{0,1:T(8,128)(2,1)S(1)}, bf16[768,292]{0,1:T(8,128)(2,1)S(1)}, u32[]{:S(2)}, u32[]{:S(2)}) collective-permute-start(bf16[768,292]{0,1:T(8,128)(2,1)S(1)} %collective-permute-done.7), channel_id=1, source_target_pairs={{4,0},{8,4},{12,8},{16,12},{20,16},{24,20},{28,24},{0,28},{5,1},{9... | collective-permute-start | bytes 1345544 | tf_op jit(solution)/shard_map/ppermute | solution.py:22
  359.5 18.3 %copy-start.1 = (bf16[3072,384]{1,0:T(8,128)(2,1)S(1)}, bf16[3072,384]{1,0:T(8,128)(2,1)}, u32[]{:S(2)}) copy-start(bf16[3072,384]{1,0:T(8,128)(2,1)} %param.11) | copy-start | bytes 7077892
Sparse Core Ops, SparseCore 0:
  9.4 83.7 all-gather.2
  94.8 80.2 all-gather.4
